TPU v7x, 128 devices: a whole 4x4x4 slice. The times are simulated.
128 devices in a mesh: ctx: 16 (over y, x_hi, core), tp: 8 (over z, x_lo).
Axes of the slice: x: 4 (x_hi: 2, x_lo: 2; x = x_hi * 2 + x_lo), y: 4, z: 4, core: 2. Of those that a mesh axis runs over, the one named last changes fastest.
Arguments:
- tokens: bfloat16 [2, 2048, 4096], P(None, 'ctx', 'tp'), may hold values from -7 to 7
- w_query: bfloat16 [4096, 2048], P(None, 'tp'), may hold values from -0.09375 to 0.09375
- w_key: bfloat16 [4096, 2048], P(None, 'tp'), may hold values from -0.09375 to 0.09375
- w_value: bfloat16 [4096, 2048], P(None, 'tp'), may hold values from -0.09375 to 0.09375
- w_out: bfloat16 [2048, 4096], P('tp'), may hold values from -0.125 to 0.125
- allowed: int32 [2, 16, 16], P(None, 'ctx'), may hold values from 0 to 1, as said below
- grad_out: bfloat16 [2, 2048, 4096], P(None, 'ctx', 'tp'), may hold values from -6 to 6
Outputs:
- attended: bfloat16 [2, 2048, 4096], P(None, 'ctx', 'tp')
- grad_tokens: bfloat16 [2, 2048, 4096], P(None, 'ctx', 'tp')
- grad_query: bfloat16 [4096, 2048], P('ctx', 'tp')
- grad_key: bfloat16 [4096, 2048], P('ctx', 'tp')
- grad_value: bfloat16 [4096, 2048], P('ctx', 'tp')
- grad_out_proj: bfloat16 [2048, 4096], P('tp', 'ctx')
Inputs may be any that keep to these rules, and one draw needn't show every extreme that they name: For each sequence b and query block i, allowed[b, i, j] is 1 exactly for j from some first block up to i: a block always sees itself and never a later block.
All inputs are finite; a program needn't handle non-finite values.
Results may differ from a plain program's by a relative error of at most 0.035.
Values may be sent and summed in bfloat16 or wider, within the bound.
A program may use at most 128 MiB of HBM per device.

v0:
```python
import jax
import jax.numpy as jnp
from jax import lax
from jax.sharding import PartitionSpec as P

HEAD_DIM = 128
FRAME = 16


def cast_half_precision(array):
    return array.astype(jnp.bfloat16)


def per_device(tokens, w_query, w_key, w_value, w_out, allowed, grad_out):
    batch_size = tokens.shape[0]
    block_len = tokens.shape[1]
    head_width = w_query.shape[1]
    heads_here = head_width // HEAD_DIM
    cycle_index = lax.axis_index("ctx")
    full_tokens, full_grads = (
        lax.all_gather(tokens, "tp", axis=2, tiled=True),
        lax.all_gather(grad_out, "tp", axis=2, tiled=True),
    )
    queries = cast_half_precision(jnp.dot(full_tokens, w_query, preferred_element_type=jnp.float32))
    key_rows = cast_half_precision(jnp.dot(full_tokens, w_key, preferred_element_type=jnp.float32))
    value_rows = cast_half_precision(
        jnp.dot(full_tokens, w_value, preferred_element_type=jnp.float32)
    )
    all_keys, all_values = (
        lax.all_gather(key_rows, "ctx", axis=1, tiled=True),
        lax.all_gather(value_rows, "ctx", axis=1, tiled=True),
    )
    window_len = all_keys.shape[1]
    query_pos = cycle_index * block_len + jnp.arange(block_len)
    key_pos = jnp.arange(window_len)
    block_ok = jnp.repeat(allowed[:, 0, :], block_len, axis=1) == 1
    visible = block_ok[:, None, :] & (
        (key_pos // FRAME)[None, None, :] <= (query_pos // FRAME)[None, :, None]
    )
    logit_scale = HEAD_DIM ** (-0.5)
    split_queries = queries.reshape(batch_size, block_len, heads_here, HEAD_DIM)
    split_keys = all_keys.reshape(batch_size, window_len, heads_here, HEAD_DIM)
    split_values = all_values.reshape(batch_size, window_len, heads_here, HEAD_DIM)
    attention_logits = (
        jnp.einsum("bqhd,bkhd->bhqk", split_queries, split_keys, preferred_element_type=jnp.float32)
        * logit_scale
    )
    attention_logits = jnp.where(visible[:, None], attention_logits, -jnp.inf)
    row_max = jnp.max(attention_logits, axis=3, keepdims=True)
    exponent = jnp.exp(attention_logits - row_max)
    row_total = jnp.sum(exponent, axis=3, keepdims=True)
    weights = exponent / row_total
    half_precision = cast_half_precision(weights)
    split_mixed = cast_half_precision(
        jnp.einsum(
            "bhqk,bkhd->bqhd", half_precision, split_values, preferred_element_type=jnp.float32
        )
    )
    mixed_heads = split_mixed.reshape(batch_size, block_len, head_width)
    out_terms = jnp.dot(mixed_heads, w_out, preferred_element_type=jnp.float32)
    attended = lax.psum_scatter(out_terms, "tp", scatter_dimension=2, tiled=True).astype(
        jnp.bfloat16
    )
    grad_heads = cast_half_precision(
        jnp.einsum("bqe,he->bqh", full_grads, w_out, preferred_element_type=jnp.float32)
    )
    split_grads = grad_heads.reshape(batch_size, block_len, heads_here, HEAD_DIM)
    again_keys, again_values = (
        lax.all_gather(key_rows, "ctx", axis=1, tiled=True),
        lax.all_gather(value_rows, "ctx", axis=1, tiled=True),
    )
    back_keys = again_keys.reshape(batch_size, window_len, heads_here, HEAD_DIM)
    back_values = again_values.reshape(batch_size, window_len, heads_here, HEAD_DIM)
    weight_gradient = jnp.einsum(
        "bqhd,bkhd->bhqk", split_grads, back_values, preferred_element_type=jnp.float32
    )
    row_inner = jnp.einsum(
        "bqhd,bqhd->bhq", split_grads, split_mixed, preferred_element_type=jnp.float32
    )[..., None]
    score_gradient = cast_half_precision(weights * (weight_gradient - row_inner) * logit_scale)
    query_gradient = cast_half_precision(
        jnp.einsum("bhqk,bkhd->bqhd", score_gradient, back_keys, preferred_element_type=jnp.float32)
    ).reshape(batch_size, block_len, head_width)
    key_part = jnp.einsum(
        "bhqk,bqhd->kbhd", score_gradient, split_queries, preferred_element_type=jnp.float32
    )
    value_part = jnp.einsum(
        "bhqk,bqhd->kbhd", half_precision, split_grads, preferred_element_type=jnp.float32
    )
    key_value = lax.psum_scatter(
        jnp.concatenate(
            (
                key_part.reshape(block_len * lax.axis_size("ctx"), batch_size, head_width),
                value_part.reshape(block_len * lax.axis_size("ctx"), batch_size, head_width),
            ),
            axis=2,
        ),
        "ctx",
        scatter_dimension=0,
        tiled=True,
    )
    key_gradient = cast_half_precision(jnp.transpose(key_value[:, :, :head_width], (1, 0, 2)))
    value_gradient = cast_half_precision(jnp.transpose(key_value[:, :, head_width:], (1, 0, 2)))
    input_terms = (
        jnp.einsum("bqh,eh->bqe", query_gradient, w_query, preferred_element_type=jnp.float32)
        + jnp.einsum("bqh,eh->bqe", key_gradient, w_key, preferred_element_type=jnp.float32)
        + jnp.einsum("bqh,eh->bqe", value_gradient, w_value, preferred_element_type=jnp.float32)
    )
    grad_tokens = lax.psum_scatter(input_terms, "tp", scatter_dimension=2, tiled=True).astype(
        jnp.bfloat16
    )
    reduced = lax.psum_scatter(
        jnp.concatenate(
            (
                jnp.einsum(
                    "bqe,bqh->eh", full_tokens, query_gradient, preferred_element_type=jnp.float32
                ),
                jnp.einsum(
                    "bqe,bqh->eh", full_tokens, key_gradient, preferred_element_type=jnp.float32
                ),
                jnp.einsum(
                    "bqe,bqh->eh", full_tokens, value_gradient, preferred_element_type=jnp.float32
                ),
                jnp.einsum(
                    "bqe,bqh->eh", full_grads, mixed_heads, preferred_element_type=jnp.float32
                ),
            ),
            axis=1,
        ),
        "ctx",
        scatter_dimension=0,
        tiled=True,
    )
    sum_query = reduced[:, :head_width]
    sum_key = reduced[:, head_width : 2 * head_width]
    sum_value = reduced[:, 2 * head_width : 3 * head_width]
    sum_out = reduced[:, 3 * head_width :]
    grad_query = cast_half_precision(sum_query)
    grad_key = cast_half_precision(sum_key)
    grad_value = cast_half_precision(sum_value)
    grad_out_proj = cast_half_precision(sum_out.T)
    return (attended, grad_tokens, grad_query, grad_key, grad_value, grad_out_proj)


def solution(mesh):
    placed = (
        P(None, "ctx", "tp"),
        P(None, "tp"),
        P(None, "tp"),
        P(None, "tp"),
        P("tp", None),
        P(None, "ctx", None),
        P(None, "ctx", "tp"),
    )
    return jax.shard_map(
        per_device,
        mesh=mesh,
        in_specs=placed,
        out_specs=(
            P(None, "ctx", "tp"),
            P(None, "ctx", "tp"),
            P("ctx", "tp"),
            P("ctx", "tp"),
            P("ctx", "tp"),
            P("tp", "ctx"),
        ),
        check_vma=False,
    )
```

profile of v0, /device:TPU:1, one launch (start us, length us, event | category | flops | bytes accessed | tf_op | source)
XLA Modules:
  0.0 693.3 jit_solution(13463311254675513724)
XLA Ops:
  7.2 0.7 all-gather.5.cloned.1.call-update
  8.0 0.7 all-gather.11.cloned.1.call-update
  8.7 56.3 %all-gather.5.cloned.1.call-done = bf16[2,128,4096]{2,1,0:T(8,128)(2,1)} async-done(((bf16[2,128,512]{2,1,0:T(8,128)(2,1)}), bf16[2,128,4096]{2,1,0:T(8,128)(2,1)}) %all-gather.5.cloned.1.call-update) | async-done | bytes 2097168 | tf_op jit(solution)/shard_map/all_gather | solution.py:21
  65.0 3.6 fusion.31
  68.7 3.6 fusion.25
  72.5 0.2 broadcast_compare_fusion
  72.7 0.3 broadcast_and_fusion
  73.0 3.0 fusion.28
  76.2 42.0 %all-gather.11.cloned.1.call-done = bf16[2,128,4096]{2,1,0:T(8,128)(2,1)} async-done(((bf16[2,128,512]{2,1,0:T(8,128)(2,1)}), bf16[2,128,4096]{2,1,0:T(8,128)(2,1)}) %all-gather.11.cloned.1.call-update) | async-done | bytes 2097168 | tf_op jit(solution)/shard_map/all_gather | solution.py:22
  118.1 2.3 fusion.34
  120.9 47.5 %all-gather.9.cloned.1.call-done = bf16[2,2048,256]{2,1,0:T(8,128)(2,1)} async-done(((bf16[2,128,256]{2,1,0:T(8,128)(2,1)}), bf16[2,2048,256]{2,1,0:T(8,128)(2,1)}) %all-gather.9.cloned.1.call-update) | async-done | bytes 2097168 | tf_op jit(solution)/shard_map/all_gather | solution.py:30
  168.4 4.0 copy.42
  172.4 5.2 fusion.50
  177.6 5.0 fusion.47
  182.6 35.0 %all-gather.7.cloned.1.call-done = bf16[2,2048,256]{2,1,0:T(8,128)(2,1)} async-done(((bf16[2,128,256]{2,1,0:T(8,128)(2,1)}), bf16[2,2048,256]{2,1,0:T(8,128)(2,1)}) %all-gather.7.cloned.1.call-update) | async-done | bytes 2097168 | tf_op jit(solution)/shard_map/all_gather | solution.py:31
  217.6 4.0 multiply_reduce_fusion
  221.5 0.7 copy-done.13
  222.2 1.1 multiply_convert_fusion
  223.3 2.7 fusion.51
  226.1 5.4 copy.23
  231.4 5.4 copy.24
  236.8 7.9 %pad_maximum_fusion.1 = f32[2048,2,512]{2,0,1:T(8,128)} fusion(f32[2048,2,256]{2,0,1:T(8,128)} %copy.24, f32[2048,2,256]{2,0,1:T(8,128)} %copy.23), kind=kLoop, calls=%fused_computation.2 | loop fusion | flops 2097152 | bytes 16777216 | tf_op jit(solution)/shard_map/concatenate | solution.py:91
  244.7 2.7 fusion.7
  247.4 0.2 reduce-scatter.9.cloned.1.call-start
  247.7 1.3 copy-done.4
  249.0 2.4 convolution_convert_fusion
  251.5 2.8 fusion.12
  254.2 90.4 %reduce-scatter.7.cloned.1.call-done = f32[128,2,512]{2,0,1:T(8,128)} async-done(((f32[2048,2,512]{2,0,1:T(8,128)}), f32[128,2,512]{2,0,1:T(8,128)}) %reduce-scatter.7.cloned.1.call-update) | async-done | bytes 524304 | tf_op jit(solution)/shard_map/reduce_scatter | solution.py:90
  344.6 1.1 convert.10
  345.7 3.1 convolution_add_fusion.1
  348.8 2.8 convolution_add_fusion
  351.7 1.5 copy-done.2
  353.2 0.7 convolution_bitcast_fusion.3
  353.9 0.9 copy-done.6
  354.8 0.7 convolution_bitcast_fusion
  355.5 0.7 convolution_bitcast_fusion.1
  356.2 0.7 convolution_bitcast_fusion.2
  357.0 6.6 pad_maximum_fusion
  363.6 74.4 %reduce-scatter.5.cloned.1.call-done = f32[2,128,512]{2,1,0:T(8,128)} async-done(((f32[2,128,4096]{2,1,0:T(8,128)}), f32[2,128,512]{2,1,0:T(8,128)}) %reduce-scatter.5.cloned.1.call-update) | async-done | bytes 524304 | tf_op jit(solution)/shard_map/reduce_scatter | solution.py:61
  438.0 1.9 convert_element_type.57
  439.9 91.8 %reduce-scatter.9.cloned.1.call-done = f32[2,128,512]{2,1,0:T(8,128)} async-done(((f32[2,128,4096]{2,1,0:T(8,128)}), f32[2,128,512]{2,1,0:T(8,128)}) %reduce-scatter.9.cloned.1.call-update) | async-done | bytes 524304 | tf_op jit(solution)/shard_map/reduce_scatter | solution.py:109
  531.6 1.8 convert_element_type.64
  533.4 148.8 %reduce-scatter.11.cloned.1.call-done = f32[256,1024]{0,1:T(8,128)} async-done(((f32[4096,1024]{0,1:T(8,128)}), f32[256,1024]{0,1:T(8,128)}) %reduce-scatter.11.cloned.1.call-update) | async-done | bytes 1048592 | tf_op jit(solution)/shard_map/reduce_scatter | solution.py:112
  682.3 1.3 convert.11
  683.5 0.7 slice_bitcast_fusion
  684.2 0.8 copy.27
  685.0 0.8 copy.28
  685.7 0.8 copy.29
  (48 shorter events, 1.1 us)
Async XLA Ops:
  7.2 111.0 %copy-start = (bf16[256,4096]{1,0:T(8,128)(2,1)S(1)}, bf16[256,4096]{1,0:T(8,128)(2,1)}, u32[]{:S(2)}) copy-start(bf16[256,4096]{1,0:T(8,128)(2,1)} %param.11) | copy-start | bytes 6291460
  7.2 57.8 %all-gather.5.cloned.1.call-start = ((), (), s32[]{:S(2)}) async-start(), calls=%async_computation.4 | async-start | bytes 2359296 | tf_op jit(solution)/shard_map/all_gather | solution.py:21
  7.9 110.2 %all-gather.11.cloned.1.call-start = ((), (), s32[]{:S(2)}) async-start(), calls=%async_computation.8 | async-start | bytes 2359296 | tf_op jit(solution)/shard_map/all_gather | solution.py:22
  8.7 159.7 %all-gather.9.cloned.1.call-start = ((), (), s32[]{:S(2)}) async-start(), calls=%async_computation.6 | async-start | bytes 2228224 | tf_op jit(solution)/shard_map/all_gather | solution.py:30
  68.6 3.7 copy-start.11
  68.6 148.9 %all-gather.7.cloned.1.call-start = ((), (), s32[]{:S(2)}) async-start(), calls=%async_computation.5 | async-start | bytes 2228224 | tf_op jit(solution)/shard_map/all_gather | solution.py:31
  72.3 272.3 %reduce-scatter.7.cloned.1.call-start = ((), (), s32[]{:S(2)}) async-start(), calls=%async_computation.9 | async-start | bytes 8912896 | tf_op jit(solution)/shard_map/reduce_scatter | solution.py:90
  120.6 57.0 %copy-start.9 = (bf16[2,128,2,128]{1,3,2,0:T(8,128)(2,1)}, bf16[2,128,2,128]{1,3,2,0:T(8,128)(2,1)S(1)}, u32[]{:S(2)}) copy-start(bf16[2,128,2,128]{1,3,2,0:T(8,128)(2,1)S(1)} %copy.22) | copy-start | bytes 393220
  182.6 39.0 %copy-start.10 = (bf16[2,128,2,128]{1,3,2,0:T(8,128)(2,1)S(1)}, bf16[2,128,2,128]{1,3,2,0:T(8,128)(2,1)}, u32[]{:S(2)}) copy-start(bf16[2,128,2,128]{1,3,2,0:T(8,128)(2,1)} %copy-done.9) | copy-start | bytes 393220
  217.6 4.0 copy-start.12
  217.6 4.7 copy-start.13
  223.3 2.7 copy-start.3
  244.7 193.3 %reduce-scatter.5.cloned.1.call-start = ((), (), s32[]{:S(2)}) async-start(), calls=%async_computation.7 | async-start | bytes 4718592 | tf_op jit(solution)/shard_map/reduce_scatter | solution.py:61
  247.4 1.6 copy-start.4
  247.4 284.2 %reduce-scatter.9.cloned.1.call-start = ((), (), s32[]{:S(2)}) async-start(), calls=%async_computation.10 | async-start | bytes 4718592 | tf_op jit(solution)/shard_map/reduce_scatter | solution.py:109
  249.0 2.5 copy-start.5
  251.5 94.2 %copy-start.7 = (bf16[4096,256]{1,0:T(8,128)(2,1)S(1)}, bf16[4096,256]{1,0:T(8,128)(2,1)}, u32[]{:S(2)}) copy-start(bf16[4096,256]{1,0:T(8,128)(2,1)} %param.9) | copy-start | bytes 6291460
  345.7 3.1 copy-start.8
  351.6 1.6 copy-start.2
  351.6 330.6 %reduce-scatter.11.cloned.1.call-start = ((), (), s32[]{:S(2)}) async-start(), calls=%async_computation.11 | async-start | bytes 17825792 | tf_op jit(solution)/shard_map/reduce_scatter | solution.py:112
  353.2 1.6 copy-start.6
  438.0 248.6 %copy-start.1 = (bf16[256,4096]{1,0:T(8,128)(2,1)S(1)}, bf16[256,4096]{1,0:T(8,128)(2,1)}, u32[]{:S(2)}) copy-start(bf16[256,4096]{1,0:T(8,128)(2,1)} %param.11) | copy-start | bytes 6291460
Sparse Core Ops, SparseCore 0:
  9.7 55.2 all-gather.4
  66.7 51.4 all-gather.10
  121.2 47.1 all-gather.8
  171.3 46.2 all-gather.6
  244.8 99.7 reduce-scatter.6
  346.9 91.0 reduce-scatter.4
  440.4 91.2 reduce-scatter.8
  535.9 146.2 reduce-scatter.10
where the time goes:
time: 694 us; the launch traced here: 693 us
  waiting for transfers between devices  588 us (85%)
  matrix products  47.1 us (7%)
  local copies, waits for them, and re-layouts  22.7 us (3%)
  other arithmetic  21.1 us (3%)
  between operations  14.4 us (2%)
    reduce_scatter x1, waiting for transfers between devices, per_device(): lax.psum_scatter(jnp.concatenate((jnp.einsum('bqe,bqh->eh', full_tokens,...  149 us
    reduce_scatter x1, waiting for transfers between devices, per_device(): lax.psum_scatter(input_terms, 'tp', scatter_dimension=2, tiled=True)  91.8 us
    reduce_scatter x1, waiting for transfers between devices, per_device(): lax.psum_scatter(jnp.concatenate((key_part.reshape(block_len * lax.axis_s...  90.4 us
    reduce_scatter x1, waiting for transfers between devices, per_device(): lax.psum_scatter(out_terms, 'tp', scatter_dimension=2, tiled=True)  74.4 us
    all_gather x1, waiting for transfers between devices, per_device(): lax.all_gather(tokens, 'tp', axis=2, tiled=True)  56.3 us
    all_gather x1, waiting for transfers between devices, per_device(): lax.all_gather(key_rows, 'ctx', axis=1, tiled=True)  47.5 us
    all_gather x1, waiting for transfers between devices, per_device(): lax.all_gather(grad_out, 'tp', axis=2, tiled=True)  42 us
    all_gather x1, waiting for transfers between devices, per_device(): lax.all_gather(value_rows, 'ctx', axis=1, tiled=True)  35 us
  transfers between devices with their start and end apart: 8, of which 8 were waited for; matrix products, arithmetic and copies ran while one was open for 8% of the time, Pallas kernels for 0%

commit v1 on v0

--- a/solution.py
+++ b/solution.py
@@ -9,6 +9,10 @@
 
 def cast_half_precision(array):
     return array.astype(jnp.bfloat16)
+
+
+def half_concatenate(pieces, axis):
+    return jnp.concatenate([cast_half_precision(piece) for piece in pieces], axis=axis)
 
 
 def per_device(tokens, w_query, w_key, w_value, w_out, allowed, grad_out):
@@ -58,19 +62,15 @@
     )
     mixed_heads = split_mixed.reshape(batch_size, block_len, head_width)
     out_terms = jnp.dot(mixed_heads, w_out, preferred_element_type=jnp.float32)
-    attended = lax.psum_scatter(out_terms, "tp", scatter_dimension=2, tiled=True).astype(
-        jnp.bfloat16
+    attended = lax.psum_scatter(
+        cast_half_precision(out_terms), "tp", scatter_dimension=2, tiled=True
     )
     grad_heads = cast_half_precision(
         jnp.einsum("bqe,he->bqh", full_grads, w_out, preferred_element_type=jnp.float32)
     )
     split_grads = grad_heads.reshape(batch_size, block_len, heads_here, HEAD_DIM)
-    again_keys, again_values = (
-        lax.all_gather(key_rows, "ctx", axis=1, tiled=True),
-        lax.all_gather(value_rows, "ctx", axis=1, tiled=True),
-    )
-    back_keys = again_keys.reshape(batch_size, window_len, heads_here, HEAD_DIM)
-    back_values = again_values.reshape(batch_size, window_len, heads_here, HEAD_DIM)
+    back_keys = split_keys
+    back_values = split_values
     weight_gradient = jnp.einsum(
         "bqhd,bkhd->bhqk", split_grads, back_values, preferred_element_type=jnp.float32
     )
@@ -88,7 +88,7 @@
         "bhqk,bqhd->kbhd", half_precision, split_grads, preferred_element_type=jnp.float32
     )
     key_value = lax.psum_scatter(
-        jnp.concatenate(
+        half_concatenate(
             (
                 key_part.reshape(block_len * lax.axis_size("ctx"), batch_size, head_width),
                 value_part.reshape(block_len * lax.axis_size("ctx"), batch_size, head_width),
@@ -106,11 +106,11 @@
         + jnp.einsum("bqh,eh->bqe", key_gradient, w_key, preferred_element_type=jnp.float32)
         + jnp.einsum("bqh,eh->bqe", value_gradient, w_value, preferred_element_type=jnp.float32)
     )
-    grad_tokens = lax.psum_scatter(input_terms, "tp", scatter_dimension=2, tiled=True).astype(
-        jnp.bfloat16
+    grad_tokens = lax.psum_scatter(
+        cast_half_precision(input_terms), "tp", scatter_dimension=2, tiled=True
     )
     reduced = lax.psum_scatter(
-        jnp.concatenate(
+        half_concatenate(
             (
                 jnp.einsum(
                     "bqe,bqh->eh", full_tokens, query_gradient, preferred_element_type=jnp.float32

time: 694 us -> 544 us (0.78)
  waiting for transfers between devices: 588 us -> 452 us
  other arithmetic: 21.1 us -> 9.07 us
    reduce_scatter x4, waiting for transfers between devices: 405 us -> 270 us  [the longest x1 93.3 us: per_device(): lax.psum_scatter(half_concatenate((jnp.einsum('bqe,bqh->eh', full_tokens,...]
    reshape x2 -> x0, local copies, waits for them, and re-layouts: 10.7 us -> none  [the longest x1 5.37 us: per_device(): value_part.reshape(block_len * lax.axis_size('ctx'), batch_size, head_width)]
    convert_element_type x1 -> x2, local copies, waits for them, and re-layouts: 0.69 us -> 7.88 us  [cast_half_precision(): return array.astype(jnp.bfloat16)]
where the time goes in v1:
time: 544 us; the launch traced here: 543 us
  waiting for transfers between devices  452 us (83%)
  matrix products  47.2 us (9%)
  local copies, waits for them, and re-layouts  19.5 us (4%)
  between operations  14.4 us (3%)
  other arithmetic  9.07 us (2%)
    reduce_scatter x1, waiting for transfers between devices, per_device(): lax.psum_scatter(half_concatenate((jnp.einsum('bqe,bqh->eh', full_tokens,...  93.3 us
    reduce_scatter x1, waiting for transfers between devices, per_device(): lax.psum_scatter(half_concatenate((key_part.reshape(block_len * lax.axis_...  70.1 us
    all_gather x1, waiting for transfers between devices, per_device(): lax.all_gather(tokens, 'tp', axis=2, tiled=True)  56.3 us
    reduce_scatter x1, waiting for transfers between devices, per_device(): lax.psum_scatter(cast_half_precision(input_terms), 'tp', scatter_dimensio...  55 us
    reduce_scatter x1, waiting for transfers between devices, per_device(): lax.psum_scatter(cast_half_precision(out_terms), 'tp', scatter_dimension=...  51.4 us
    all_gather x1, waiting for transfers between devices, per_device(): lax.all_gather(key_rows, 'ctx', axis=1, tiled=True)  47.5 us
    all_gather x1, waiting for transfers between devices, per_device(): lax.all_gather(grad_out, 'tp', axis=2, tiled=True)  42 us
    all_gather x1, waiting for transfers between devices, per_device(): lax.all_gather(value_rows, 'ctx', axis=1, tiled=True)  35.5 us
  transfers between devices with their start and end apart: 8, of which 8 were waited for; matrix products, arithmetic and copies ran while one was open for 8% of the time, Pallas kernels for 0%

profile of v1, /device:TPU:1, one launch (start us, length us, event | category | flops | bytes accessed | tf_op | source)
XLA Modules:
  0.0 543.1 jit_solution(1655865423010924809)
XLA Ops:
  7.2 0.7 all-gather.5.cloned.1.call-update
  8.0 0.7 all-gather.11.cloned.1.call-update
  8.7 56.3 %all-gather.5.cloned.1.call-done = bf16[2,128,4096]{2,1,0:T(8,128)(2,1)} async-done(((bf16[2,128,512]{2,1,0:T(8,128)(2,1)}), bf16[2,128,4096]{2,1,0:T(8,128)(2,1)}) %all-gather.5.cloned.1.call-update) | async-done | bytes 2097168 | tf_op jit(solution)/shard_map/all_gather | solution.py:25
  65.0 3.6 fusion.39
  68.7 3.6 fusion.33
  72.5 0.2 broadcast_compare_fusion
  72.7 0.3 broadcast_and_fusion
  73.0 3.0 fusion.36
  76.0 0.1 copy.41
  76.2 42.0 %all-gather.11.cloned.1.call-done = bf16[2,128,4096]{2,1,0:T(8,128)(2,1)} async-done(((bf16[2,128,512]{2,1,0:T(8,128)(2,1)}), bf16[2,128,4096]{2,1,0:T(8,128)(2,1)}) %all-gather.11.cloned.1.call-update) | async-done | bytes 2097168 | tf_op jit(solution)/shard_map/all_gather | solution.py:26
  118.1 2.3 fusion.42
  120.5 0.1 copy.22
  120.6 0.1 bitcast_convert_fusion
  120.7 0.1 copy.36
  120.9 47.5 %all-gather.9.cloned.1.call-done = bf16[2,2048,256]{2,1,0:T(8,128)(2,1)} async-done(((bf16[2,128,256]{2,1,0:T(8,128)(2,1)}), bf16[2,2048,256]{2,1,0:T(8,128)(2,1)}) %all-gather.9.cloned.1.call-update) | async-done | bytes 2097168 | tf_op jit(solution)/shard_map/all_gather | solution.py:34
  168.4 4.0 copy.42
  172.4 5.3 fusion.57
  177.7 4.4 convolution_convert_fusion.1
  182.1 35.5 %all-gather.7.cloned.1.call-done = bf16[2,2048,256]{2,1,0:T(8,128)(2,1)} async-done(((bf16[2,128,256]{2,1,0:T(8,128)(2,1)}), bf16[2,2048,256]{2,1,0:T(8,128)(2,1)}) %all-gather.7.cloned.1.call-update) | async-done | bytes 2097168 | tf_op jit(solution)/shard_map/all_gather | solution.py:35
  217.6 4.0 multiply_reduce_fusion
  221.5 0.7 copy-done.14
  222.2 1.1 multiply_convert_fusion
  223.3 2.0 convolution_convert_fusion.2
  225.4 3.9 copy.23
  229.3 3.9 copy.24
  233.3 4.5 pad_maximum_fusion.1
  237.8 0.2 reduce-scatter.11.cloned.1.call-start
  238.0 3.1 convolution_convert_fusion.3
  241.1 2.1 fusion.9
  243.2 2.0 fusion.6
  245.2 70.1 %reduce-scatter.7.cloned.1.call-done = bf16[128,2,512]{2,0,1:T(8,128)(2,1)} async-done(((bf16[2048,2,512]{2,0,1:T(8,128)(2,1)}), bf16[128,2,512]{2,0,1:T(8,128)(2,1)}) %reduce-scatter.7.cloned.1.call-update) | async-done | bytes 262160 | tf_op jit(solution)/shard_map/reduce_scatter | solution.py:90
  315.4 2.5 fusion.7
  318.0 0.7 fusion.8
  318.7 0.8 copy-done.4
  319.5 0.6 copy-done.5
  320.2 4.0 pad_maximum_fusion
  324.2 2.1 convolution_convert_fusion
  326.4 2.5 fusion.20
  328.9 0.7 convolution_add_fusion.1
  329.7 0.8 copy-done.8
  330.5 2.1 fusion.1
  332.6 93.3 %reduce-scatter.11.cloned.1.call-done = bf16[256,1024]{0,1:T(8,128)(2,1)} async-done(((bf16[4096,1024]{0,1:T(8,128)(2,1)}), bf16[256,1024]{0,1:T(8,128)(2,1)}) %reduce-scatter.11.cloned.1.call-update) | async-done | bytes 524304 | tf_op jit(solution)/shard_map/reduce_scatter | solution.py:112
  425.9 1.8 slice_bitcast_fusion
  427.7 0.8 copy.27
  428.4 0.8 copy.28
  429.2 0.8 copy.29
  430.0 51.4 %reduce-scatter.5.cloned.1.call-done = bf16[2,128,512]{2,1,0:T(8,128)(2,1)} async-done(((bf16[2,128,4096]{2,1,0:T(8,128)(2,1)}), bf16[2,128,512]{2,1,0:T(8,128)(2,1)}) %reduce-scatter.5.cloned.1.call-update) | async-done | bytes 262160 | tf_op jit(solution)/shard_map/reduce_scatter | solution.py:65
  481.3 55.0 %reduce-scatter.9.cloned.1.call-done = bf16[2,128,512]{2,1,0:T(8,128)(2,1)} async-done(((bf16[2,128,4096]{2,1,0:T(8,128)(2,1)}), bf16[2,128,512]{2,1,0:T(8,128)(2,1)}) %reduce-scatter.9.cloned.1.call-update) | async-done | bytes 262160 | tf_op jit(solution)/shard_map/reduce_scatter | solution.py:109
  (46 shorter events, 0.6 us)
Async XLA Ops:
  7.2 111.0 %copy-start = (bf16[256,4096]{1,0:T(8,128)(2,1)S(1)}, bf16[256,4096]{1,0:T(8,128)(2,1)}, u32[]{:S(2)}) copy-start(bf16[256,4096]{1,0:T(8,128)(2,1)} %param.11) | copy-start | bytes 6291460
  7.2 57.8 %all-gather.5.cloned.1.call-start = ((), (), s32[]{:S(2)}) async-start(), calls=%async_computation.4 | async-start | bytes 2359296 | tf_op jit(solution)/shard_map/all_gather | solution.py:25
  7.9 110.2 %all-gather.11.cloned.1.call-start = ((), (), s32[]{:S(2)}) async-start(), calls=%async_computation.8 | async-start | bytes 2359296 | tf_op jit(solution)/shard_map/all_gather | solution.py:26
  8.7 159.7 %all-gather.9.cloned.1.call-start = ((), (), s32[]{:S(2)}) async-start(), calls=%async_computation.6 | async-start | bytes 2228224 | tf_op jit(solution)/shard_map/all_gather | solution.py:34
  68.6 3.7 copy-start.12
  68.6 148.9 %all-gather.7.cloned.1.call-start = ((), (), s32[]{:S(2)}) async-start(), calls=%async_computation.5 | async-start | bytes 2228224 | tf_op jit(solution)/shard_map/all_gather | solution.py:35
  72.3 243.1 %reduce-scatter.7.cloned.1.call-start = ((), (), s32[]{:S(2)}) async-start(), calls=%async_computation.9 | async-start | bytes 4456448 | tf_op jit(solution)/shard_map/reduce_scatter | solution.py:90
  120.6 57.1 %copy-start.10 = (bf16[2,128,2,128]{1,3,2,0:T(8,128)(2,1)}, bf16[2,128,2,128]{1,3,2,0:T(8,128)(2,1)S(1)}, u32[]{:S(2)}) copy-start(bf16[2,128,2,128]{1,3,2,0:T(8,128)(2,1)S(1)} %copy.22) | copy-start | bytes 393220
  182.1 39.4 %copy-start.11 = (bf16[2,128,2,128]{1,3,2,0:T(8,128)(2,1)S(1)}, bf16[2,128,2,128]{1,3,2,0:T(8,128)(2,1)}, u32[]{:S(2)}) copy-start(bf16[2,128,2,128]{1,3,2,0:T(8,128)(2,1)} %copy-done.10) | copy-start | bytes 393220
  217.6 4.0 copy-start.13
  217.6 4.7 copy-start.14
  223.3 2.0 copy-start.3
  237.8 188.1 %reduce-scatter.11.cloned.1.call-start = ((), (), s32[]{:S(2)}) async-start(), calls=%async_computation.11 | async-start | bytes 8912896 | tf_op jit(solution)/shard_map/reduce_scatter | solution.py:112
  238.0 3.1 copy-start.1
  241.1 2.1 copy-start.6
  315.4 2.5 copy-start.2
  315.4 2.6 copy-start.9
  317.9 1.6 copy-start.4
  318.0 2.2 copy-start.5
  324.1 157.2 %reduce-scatter.5.cloned.1.call-start = ((), (), s32[]{:S(2)}) async-start(), calls=%async_computation.7 | async-start | bytes 2359296 | tf_op jit(solution)/shard_map/reduce_scatter | solution.py:65
  326.3 209.9 %reduce-scatter.9.cloned.1.call-start = ((), (), s32[]{:S(2)}) async-start(), calls=%async_computation.10 | async-start | bytes 2359296 | tf_op jit(solution)/shard_map/reduce_scatter | solution.py:109
  326.4 2.5 copy-start.7
  328.9 1.6 copy-start.8
Sparse Core Ops, SparseCore 0:
  9.7 55.2 all-gather.4
  66.7 51.4 all-gather.10
  121.2 47.1 all-gather.8
  171.3 46.2 all-gather.6
  237.9 77.4 reduce-scatter.6
  324.3 101.5 reduce-scatter.10
  429.0 52.2 reduce-scatter.4
  484.4 51.7 reduce-scatter.8

commit v2 on v1

v2 whole, which is shorter than its diff:
```python
import functools

import jax
import jax.numpy as jnp
from jax import lax
from jax.experimental import pallas as pl
from jax.experimental.pallas import tpu as pltpu
from jax.sharding import PartitionSpec as P

HEAD_DIM = 128
FRAME = 16
MESH = pl.DeviceIdType.MESH
BF = jnp.bfloat16
F32 = jnp.float32

ORDER = ((2, 1), (1, 1), (3, 1), (1, 0), (3, 0), (2, 0), (0, 1), (0, 0))
INDEX = {offset: k for k, offset in enumerate(ORDER)}
GATHER_COPIES = 7
SCATTER_COPIES = 7


def dot(a, b):
    return jnp.dot(a, b, preferred_element_type=F32)


def dot_nt(a, b):
    return lax.dot_general(a, b, (((1,), (1,)), ((), ())), preferred_element_type=F32)


def dot_tn(a, b):
    return lax.dot_general(a, b, (((0,), (0,)), ((), ())), preferred_element_type=F32)


class Copies:
    def __init__(self, send_sems, recv_sems):
        self.send_sems, self.recv_sems = send_sems, recv_sems
        self.used = 0
        self.started = []

    def start(self, src, dst, device):
        k = self.used
        self.used += 1
        copy = pltpu.make_async_remote_copy(
            src_ref=src,
            dst_ref=dst,
            send_sem=self.send_sems.at[k],
            recv_sem=self.recv_sems.at[k],
            device_id=device,
            device_id_type=MESH,
        )
        copy.start()
        self.started.append(copy)
        return copy

    def finish(self):
        for copy in self.started:
            copy.wait_send()


class Gather:
    def __init__(self, copies, peer, own, slot, landing):
        self.copies, self.peer, self.slot, self.landing = copies, peer, slot, landing
        go = copies.start
        self.pair = go(own, landing(0, 1, 0, 0), peer(0, 1))
        self.far = go(own, landing(2, 0, 0, 0), peer(2, 0))
        self.up = go(own, landing(1, 0, 0, 0), peer(1, 0))
        self.down = go(own, landing(3, 0, 0, 0), peer(3, 0))

    def forward_pair(self):
        self.pair.wait_recv()
        go = self.copies.start
        self.up_pair = go(self.slot(0, 1), self.landing(1, 0, 0, 1), self.peer(1, 0))
        self.down_pair = go(self.slot(0, 1), self.landing(3, 0, 0, 1), self.peer(3, 0))

    def forward_far(self):
        self.far.wait_recv()
        self.far_pair = self.copies.start(
            self.slot(2, 0), self.landing(0, 1, 2, 0), self.peer(0, 1)
        )


class Scatter:
    def __init__(self, copies, peer, parts, landed, add):
        self.copies, self.peer, self.parts, self.landed, self.add = copies, peer, parts, landed, add

    def send(self, k):
        ring, pair = ORDER[k]
        to = self.peer(0, 1) if ring == 2 else self.peer(ring, 0)
        copy = self.copies.start(self.parts.at[k], self.landed.at[k], to)
        setattr(self, ("far_pair", "up_pair", "down_pair", "up", "down")[k], copy)

    def relay_far(self):
        self.far_pair.wait_recv()
        self.add(self.parts.at[5], (self.parts.at[5], self.landed.at[0]))
        self.far = self.copies.start(self.parts.at[5], self.landed.at[5], self.peer(2, 0))

    def relay_pair(self):
        self.up_pair.wait_recv()
        self.down_pair.wait_recv()
        self.add(
            self.parts.at[6], (self.parts.at[6], self.landed.at[1], self.landed.at[2])
        )
        self.pair = self.copies.start(self.parts.at[6], self.landed.at[6], self.peer(0, 1))

    def finish(self, store):
        for copy in (self.up, self.down, self.far, self.pair):
            copy.wait_recv()
        store(
            (
                self.parts.at[7],
                self.landed.at[3],
                self.landed.at[4],
                self.landed.at[5],
                self.landed.at[6],
            )
        )


def summed(refs, where):
    total = refs[0][where].astype(F32)
    for ref in refs[1:]:
        total = total + ref[where].astype(F32)
    return total


def add_rows(step):
    def add(dst, refs):
        def body(i, carry):
            where = (pl.ds(pl.multiple_of(i * step, step), step), slice(None))
            dst[where] = summed(refs, where).astype(dst.dtype)
            return carry

        lax.fori_loop(0, dst.shape[0] // step, body, 0)

    return add


def add_lead(dst, refs):
    def body(i, carry):
        dst[i] = summed(refs, i).astype(dst.dtype)
        return carry

    lax.fori_loop(0, dst.shape[0], body, 0)


def kernel(
    first_ref,
    tok_ref,
    wq_hbm,
    wk_hbm,
    wv_hbm,
    wo_hbm,
    gout_ref,
    att_out,
    dtok_out,
    gq_out,
    gk_out,
    gv_out,
    go_out,
    wq,
    wk,
    wv,
    wo,
    x_all,
    g_all,
    x_sib,
    g_sib,
    xt_all,
    qkv_acc,
    do_acc,
    q_own,
    do_own,
    kv,
    prob,
    mixed,
    mixed_sib,
    grads,
    grads_sib,
    kv_mate,
    kv_mate_in,
    att_parts,
    att_in,
    dkv_parts,
    dkv_in,
    dtok_parts,
    dtok_in,
    wo_parts,
    wo_in,
    wq_parts,
    wq_in,
    wkv_parts,
    wkv_in,
    send_sems,
    recv_sems,
    local_sems,
):
    ctx, tp = lax.axis_index("ctx"), lax.axis_index("tp")
    y, xh, core = ctx // 4, (ctx // 2) % 2, ctx % 2
    z, xl = tp // 2, tp % 2
    width = 512
    half = 256
    scale = HEAD_DIM ** (-0.5)

    def tp_peer(ring, pair):
        return (ctx, ((z + ring) % 4) * 2 + (xl + pair) % 2)

    def tp_at(ring, pair):
        return ((z + ring) % 4) * 2 + (xl + pair) % 2

    def ctx_peer(ring, pair):
        return (((y + ring) % 4) * 4 + ((xh + pair) % 2) * 2 + core, tp)

    def chip_at(ring, pair):
        return ((y + ring) % 4) * 2 + (xh + pair) % 2

    mate = (ctx + 1 - 2 * core, tp)

    local = [
        pltpu.make_async_copy(src, dst, local_sems.at[k])
        for k, (src, dst) in enumerate(
            (
                (tok_ref, x_all.at[tp]),
                (wq_hbm, wq),
                (wk_hbm, wk),
                (wv_hbm, wv),
                (wo_hbm, wo),
                (gout_ref, g_all.at[tp]),
            )
        )
    ]
    for copy in local:
        copy.start()

    barrier = pltpu.get_barrier_semaphore()
    neighbours = [
        at(ring, pair)
        for at in (tp_peer, ctx_peer)
        for ring, pair in ((0, 1), (1, 0), (2, 0), (3, 0))
    ] + [mate]
    for device in neighbours:
        pl.semaphore_signal(barrier, inc=1, device_id=device, device_id_type=MESH)
    pl.semaphore_wait(barrier, len(neighbours))

    copies = Copies(send_sems, recv_sems)

    def tp_gather(own, slots):
        return Gather(
            copies,
            tp_peer,
            own,
            lambda ring, pair: slots.at[tp_at(ring, pair)],
            lambda to_ring, to_pair, ring, pair: slots.at[tp_at(ring, pair)],
        )

    def ctx_landing(to_ring, to_pair, ring, pair):
        return kv.at[0, INDEX[((ring - to_ring) % 4, (pair + to_pair) % 2)]]

    tokens = tp_gather(tok_ref, x_all)

    def project(slot, first=False):
        x = x_all[slot]
        rows = pl.ds(pl.multiple_of(slot * width, width), width)
        for k, w in enumerate((wq, wk, wv)):
            term = dot(x, w[rows, :])
            where = (slice(None), slice(k * half, (k + 1) * half))
            if first:
                qkv_acc[where] = term
            else:
                qkv_acc[where] += term

    for copy in local[:4]:
        copy.wait()
    project(tp, first=True)
    tokens.forward_pair()
    project(tp_at(0, 1))
    tokens.forward_far()
    tokens.up.wait_recv()
    tokens.down.wait_recv()
    cotangents = tp_gather(gout_ref, g_all)
    project(tp_at(2, 0))
    project(tp_at(1, 0))
    project(tp_at(3, 0))
    tokens.up_pair.wait_recv()
    tokens.down_pair.wait_recv()
    project(tp_at(1, 1))
    project(tp_at(3, 1))
    tokens.far_pair.wait_recv()
    project(tp_at(2, 1))

    own_kv = kv.at[0, INDEX[(0, 0)]]
    for p in range(4):
        b, h = p // 2, p % 2
        rows = slice(b * 128, (b + 1) * 128)
        q_own[p] = qkv_acc[rows, h * 128 : (h + 1) * 128].astype(BF)
        own_kv[2 * p] = qkv_acc[rows, half + h * 128 : half + (h + 1) * 128].astype(BF)
        own_kv[2 * p + 1] = qkv_acc[
            rows, 2 * half + h * 128 : 2 * half + (h + 1) * 128
        ].astype(BF)

    rows_kv = Gather(
        copies, ctx_peer, own_kv, lambda ring, pair: kv.at[0, INDEX[(ring, pair)]], ctx_landing
    )
    shared = []

    def share(ring, pair):
        k = INDEX[(ring, pair)]
        shared.append(copies.start(kv.at[0, k], kv.at[1, k], mate))

    share(0, 0)
    other_half = pl.ds(pl.multiple_of((1 - core) * half, half), half)
    my_half = pl.ds(pl.multiple_of(core * half, half), half)
    x_half = copies.start(x_all.at[:, :, other_half], x_sib, mate)
    local[5].wait()
    cotangents.forward_pair()
    rows_kv.forward_pair()
    share(0, 1)
    cotangents.forward_far()
    x_half.wait_recv()

    def transpose_block(k, carry):
        xt_all[k, :, :half] = x_all[k, :, my_half].T
        xt_all[k, :, half:] = x_sib[k].T
        return carry

    lax.fori_loop(0, 8, transpose_block, 0)
    rows_kv.forward_far()
    share(2, 0)
    cotangents.up.wait_recv()
    cotangents.down.wait_recv()
    local[4].wait()

    def pull_back(slot, first=False):
        columns = pl.ds(pl.multiple_of(slot * width, width), width)
        term = dot_nt(g_all[slot], wo[:, columns])
        if first:
            do_acc[...] = term
        else:
            do_acc[...] += term

    pull_back(tp, first=True)
    for offset in ((0, 1), (2, 0), (1, 0), (3, 0)):
        pull_back(tp_at(*offset))
    rows_kv.up.wait_recv()
    share(3, 0)
    rows_kv.down.wait_recv()
    share(1, 0)
    cotangents.up_pair.wait_recv()
    cotangents.down_pair.wait_recv()
    pull_back(tp_at(1, 1))
    pull_back(tp_at(3, 1))
    cotangents.far_pair.wait_recv()
    pull_back(tp_at(2, 1))
    g_half = copies.start(g_all.at[:, :, other_half], g_sib, mate)
    for p in range(4):
        b, h = p // 2, p % 2
        do_own[p] = do_acc[b * 128 : (b + 1) * 128, h * 128 : (h + 1) * 128].astype(BF)
    rows_kv.up_pair.wait_recv()
    share(3, 1)
    rows_kv.down_pair.wait_recv()
    share(1, 1)
    rows_kv.far_pair.wait_recv()
    share(2, 1)
    for copy in shared:
        copy.wait_recv()

    key_frame = lax.broadcasted_iota(jnp.int32, (128, 128), 0) // FRAME
    frame_gap = key_frame - lax.broadcasted_iota(jnp.int32, (128, 128), 1) // FRAME
    frames = 128 // FRAME
    blocks = [
        [2 * chip_at(*ORDER[k]) + (core if d == 0 else 1 - core) for k in range(8)]
        for d in range(2)
    ]

    def forward(p, carry):
        b = p // 2
        q = q_own[p]
        lowest = first_ref[b]
        tops = []
        for d in range(2):
            keys = kv[d, :, 2 * p].reshape(8 * 128, HEAD_DIM)
            logits = (dot_nt(keys, q) * scale).reshape(8, 128, 128)
            for k in range(8):
                block = blocks[d][k]
                visible = (frame_gap <= (ctx - block) * frames) & (
                    key_frame >= (lowest - block) * frames
                )
                masked = jnp.where(visible, logits[k], -jnp.inf)
                prob[p, d, k] = masked
                tops.append(jnp.max(masked, axis=0, keepdims=True))
        top = functools.reduce(jnp.maximum, tops)
        total = jnp.zeros((1, 128), F32)
        for d in range(2):
            for k in range(8):
                exponent = jnp.exp(prob[p, d, k] - top)
                prob[p, d, k] = exponent
                total = total + jnp.sum(exponent, axis=0, keepdims=True)
        inverse = 1.0 / total
        out = jnp.zeros((128, HEAD_DIM), F32)
        for d in range(2):
            weights = prob[p, d] * inverse
            prob[p, d] = weights
            values = kv[d, :, 2 * p + 1].reshape(8 * 128, HEAD_DIM)
            out = out + dot_tn(weights.reshape(8 * 128, 128).astype(BF), values)
        rows = pl.ds(pl.multiple_of(b * 128, 128), 128)
        columns = pl.ds(pl.multiple_of((p % 2) * 128, 128), 128)
        mixed[rows, columns] = out.astype(BF)
        return carry

    lax.fori_loop(0, 4, forward, 0)

    mixed_copy = copies.start(mixed, mixed_sib, mate)
    attended = Scatter(copies, tp_peer, att_parts, att_in, add_rows(64))

    def out_part(k):
        columns = pl.ds(pl.multiple_of(tp_at(*ORDER[k]) * width, width), width)
        att_parts[k] = dot(mixed[...], wo[:, columns]).astype(BF)

    for k in range(8):
        out_part(k)
        if k < 5:
            attended.send(k)
    mixed_copy.wait_recv()
    g_half.wait_recv()

    out_grads = Scatter(copies, ctx_peer, wo_parts, wo_in, add_rows(64))
    for k in range(8):
        chip = chip_at(*ORDER[k])
        wo_parts[k] = (
            dot_tn(mixed[...], g_all[chip, :, my_half]) + dot_tn(mixed_sib[...], g_sib[chip])
        ).astype(BF)
        if k < 5:
            out_grads.send(k)

    def backward(d, out):
        def body(p, carry):
            rows = pl.ds(pl.multiple_of((p // 2) * 128, 128), 128)
            columns = pl.ds(pl.multiple_of((p % 2) * 128, 128), 128)
            q, do = q_own[p], do_own[p]
            inner = lax.dot_general(
                jnp.ones((8, HEAD_DIM), F32),
                do.astype(F32) * mixed[rows, columns].astype(F32),
                (((1,), (1,)), ((), ())),
                precision=lax.Precision.HIGHEST,
                preferred_element_type=F32,
            )[0:1]
            keys = kv[d, :, 2 * p].reshape(8 * 128, HEAD_DIM)
            values = kv[d, :, 2 * p + 1].reshape(8 * 128, HEAD_DIM)
            weights = prob[p, d].reshape(8 * 128, 128)
            slopes = (weights * (dot_nt(values, do) - inner) * scale).astype(BF)
            out[:, 2 * p] = dot(slopes, q).astype(BF).reshape(8, 128, HEAD_DIM)
            out[:, 2 * p + 1] = dot(weights.astype(BF), do).astype(BF).reshape(8, 128, HEAD_DIM)
            term = dot_tn(slopes, keys)
            if d == 1:
                do_acc[rows, columns] = term
            else:
                do_acc[rows, columns] += term
            return carry

        lax.fori_loop(0, 4, body, 0)

    backward(1, kv_mate)
    mate_copy = copies.start(kv_mate, kv_mate_in, mate)
    backward(0, dkv_parts)
    grads[:, :half] = do_acc[...].astype(BF)
    dq_copy = copies.start(grads.at[:, pl.ds(0, half)], grads_sib.at[:, pl.ds(0, half)], mate)
    mate_copy.wait_recv()
    kv_sums = Scatter(copies, ctx_peer, dkv_parts, dkv_in, add_lead)
    for k in range(8):
        add_lead(dkv_parts.at[k], (dkv_parts.at[k], kv_mate_in.at[k]))
        if k < 5:
            kv_sums.send(k)
    attended.relay_far()
    attended.relay_pair()
    out_grads.relay_far()
    out_grads.relay_pair()

    dq_copy.wait_recv()
    query_grads = Scatter(copies, ctx_peer, wq_parts, wq_in, add_rows(64))
    for k in range(8):
        chip = chip_at(*ORDER[k])
        wq_parts[k] = (
            dot(xt_all[chip, :, :half], grads[:, :half])
            + dot(xt_all[chip, :, half:], grads_sib[:, :half])
        ).astype(BF)
        if k < 5 and k != 0:
            query_grads.send(k)
    query_grads.send(0)
    kv_sums.relay_far()
    kv_sums.relay_pair()

    def store_rows(out):
        return lambda refs: add_rows(64)(out, refs)

    attended.finish(store_rows(att_out))
    out_grads.finish(store_rows(go_out))

    def store_kv(refs):
        for p in range(4):
            b, h = p // 2, p % 2
            for which in range(2):
                at = (1 + which) * half + h * 128
                grads[b * 128 : (b + 1) * 128, at : at + 128] = summed(
                    refs, 2 * p + which
                ).astype(BF)

    kv_sums.finish(store_kv)
    kv_columns = pl.ds(half, 2 * half)
    dkv_copy = copies.start(grads.at[:, kv_columns], grads_sib.at[:, kv_columns], mate)

    token_grads = Scatter(copies, tp_peer, dtok_parts, dtok_in, add_rows(64))
    for k in range(8):
        rows = pl.ds(pl.multiple_of(tp_at(*ORDER[k]) * width, width), width)
        dtok_parts[k] = (
            dot_nt(grads[:, :half], wq[rows, :])
            + dot_nt(grads[:, half : 2 * half], wk[rows, :])
            + dot_nt(grads[:, 2 * half :], wv[rows, :])
        ).astype(BF)
        if k < 5:
            token_grads.send(k)

    dkv_copy.wait_recv()
    kv_grads = Scatter(copies, ctx_peer, wkv_parts, wkv_in, add_rows(64))
    for k in range(8):
        chip = chip_at(*ORDER[k])
        wkv_parts[k] = (
            dot(xt_all[chip, :, :half], grads[:, half:])
            + dot(xt_all[chip, :, half:], grads_sib[:, half:])
        ).astype(BF)
        if k < 5:
            kv_grads.send(k)
    query_grads.relay_far()
    query_grads.relay_pair()
    token_grads.relay_far()
    token_grads.relay_pair()
    kv_grads.relay_far()
    kv_grads.relay_pair()
    query_grads.finish(store_rows(gq_out))
    token_grads.finish(store_rows(dtok_out))

    def store_pair(refs):
        def body(i, carry):
            rows = pl.ds(pl.multiple_of(i * 64, 64), 64)
            total = summed(refs, (rows, slice(None))).astype(BF)
            gk_out[rows, :] = total[:, :half]
            gv_out[rows, :] = total[:, half:]
            return carry

        lax.fori_loop(0, 4, body, 0)

    kv_grads.finish(store_pair)
    copies.finish()


N_COPIES = 3 * GATHER_COPIES + 6 * SCATTER_COPIES + 8 + 6


def per_device(tokens, w_query, w_key, w_value, w_out, allowed, grad_out):
    batch, block, width = tokens.shape
    rows = batch * block
    head_width = w_query.shape[1]
    first = lax.axis_index("ctx") + 1 - jnp.sum(allowed[:, 0, :], axis=1, dtype=jnp.int32)
    vmem = pl.BlockSpec(memory_space=pltpu.VMEM)
    hbm = pl.BlockSpec(memory_space=pl.ANY)

    def halves(*shape):
        return pltpu.VMEM(shape, BF)

    def pair(*shape):
        return [halves(8, *shape), halves(7, *shape)]

    outs = pl.pallas_call(
        kernel,
        out_shape=[jax.ShapeDtypeStruct((rows, width), BF)] * 2
        + [jax.ShapeDtypeStruct((head_width, head_width), BF)] * 4,
        in_specs=[pl.BlockSpec(memory_space=pltpu.SMEM)] + [hbm] * 6,
        out_specs=[vmem] * 6,
        scratch_shapes=[
            halves(4096, 256),
            halves(4096, 256),
            halves(4096, 256),
            halves(256, 4096),
            halves(8, 256, 512),
            halves(8, 256, 512),
            halves(8, 256, 256),
            halves(8, 256, 256),
            halves(8, 256, 512),
            pltpu.VMEM((256, 768), F32),
            pltpu.VMEM((256, 256), F32),
            halves(4, 128, 128),
            halves(4, 128, 128),
            halves(2, 8, 8, 128, 128),
            pltpu.VMEM((4, 2, 8, 128, 128), F32),
            halves(256, 256),
            halves(256, 256),
            halves(256, 768),
            halves(256, 768),
            halves(8, 8, 128, 128),
            halves(8, 8, 128, 128),
            *pair(256, 512),
            *pair(8, 128, 128),
            *pair(256, 512),
            *pair(256, 256),
            *pair(256, 256),
            *pair(256, 512),
            pltpu.SemaphoreType.DMA((N_COPIES,)),
            pltpu.SemaphoreType.DMA((N_COPIES,)),
            pltpu.SemaphoreType.DMA((6,)),
        ],
        compiler_params=pltpu.CompilerParams(
            collective_id=0, has_side_effects=True, vmem_limit_bytes=60 * 2**20
        ),
    )(
        first,
        tokens.reshape(rows, width),
        w_query,
        w_key,
        w_value,
        w_out,
        grad_out.reshape(rows, width),
    )
    attended, grad_tokens, *weight_grads = outs
    return (
        attended.reshape(batch, block, width),
        grad_tokens.reshape(batch, block, width),
        *weight_grads,
    )


def solution(mesh):
    placed = (
        P(None, "ctx", "tp"),
        P(None, "tp"),
        P(None, "tp"),
        P(None, "tp"),
        P("tp", None),
        P(None, "ctx", None),
        P(None, "ctx", "tp"),
    )
    return jax.shard_map(
        per_device,
        mesh=mesh,
        in_specs=placed,
        out_specs=(
            P(None, "ctx", "tp"),
            P(None, "ctx", "tp"),
            P("ctx", "tp"),
            P("ctx", "tp"),
            P("ctx", "tp"),
            P("tp", "ctx"),
        ),
        check_vma=False,
    )
```

time: 544 us -> 135 us (0.25)
  waiting for transfers between devices: 452 us -> 0 us
  Pallas kernels: 0 us -> 122 us
  matrix products: 47.2 us -> 0 us
  between operations: 14.4 us -> 0.65 us
  local copies, waits for them, and re-layouts: 19.5 us -> 9.61 us
  other arithmetic: 9.07 us -> 1.33 us
    reduce_scatter x4 -> x0, waiting for transfers between devices: 270 us -> none  [the longest x1 93.3 us: per_device(): lax.psum_scatter(half_concatenate((jnp.einsum('bqe,bqh->eh', full_tokens,...]
    all_gather x4 -> x0, waiting for transfers between devices: 181 us -> none  [the longest x1 56.3 us: per_device(): lax.all_gather(tokens, 'tp', axis=2, tiled=True)]
    pallas_call x0 -> x1, Pallas kernels: none -> 122 us  [per_device(): pl.pallas_call(kernel, out_shape=[jax.ShapeDtypeStruct((rows, width), BF)...]
    dot_general x17 -> x0, matrix products: 41.9 us -> none  [the longest x1 4.41 us: per_device(): jnp.einsum('bhqk,bqhd->kbhd', half_precision, split_grads, preferred_elem...]
    concatenate x2 -> x0, other arithmetic: 8.44 us -> none  [half_concatenate(): jnp.concatenate([cast_half_precision(piece) for piece in pieces], axis=axis)]
    convert_element_type x2 -> x0, local copies, waits for them, and re-layouts: 7.88 us -> none  [cast_half_precision(): return array.astype(jnp.bfloat16)]
  transfers between devices with their start and end apart: 8 -> 0, of which waited for: 8 -> 0; matrix products, arithmetic and copies ran while one was open for 8% -> 0% of each run, Pallas kernels for 0% -> 0%
where the time goes in v2:
time: 135 us; the launch traced here: 134 us
  Pallas kernels  122 us (90%)
  local copies, waits for them, and re-layouts  9.61 us (7%)
    pallas_call x1, Pallas kernels, per_device(): pl.pallas_call(kernel, out_shape=[jax.ShapeDtypeStruct((rows, width), BF)...  122 us
    unnamed x6, local copies, waits for them, and re-layouts  9.61 us

profile of v2, /device:TPU:1, one launch (start us, length us, event | category | flops | bytes accessed | tf_op | source)
XLA Modules:
  0.0 133.9 jit_solution(662899758340270139)
XLA Ops:
  0.6 0.8 reduce_sum.9
  1.4 0.5 broadcast_subtract_fusion.first_ref
  2.0 122.3 %shard_map.118 = (bf16[256,512]{1,0:T(8,128)(2,1)}, bf16[256,512]{1,0:T(8,128)(2,1)}, bf16[256,256]{1,0:T(8,128)(2,1)}, bf16[256,256]{1,0:T(8,128)(2,1)}, bf16[2...) custom-call(s32[2]{0:T(128)} %broadcast_subtract_fusion.first_ref, bf16[256,512]{1,0:T(8,128)(2,1)} %bitcast.4, ...), custom_call_target="tpu_custom_call" | custom-call | tf_op jit(solution)/shard_map/pallas_call | solution.py:571
  124.3 1.7 %copy.19 = bf16[2,128,512]{2,1,0:T(8,128)(2,1)} copy(bf16[2,128,512]{2,1,0:T(8,128)(2,1)} %bitcast.7) | data formatting | bytes 524288
  126.0 1.7 %copy.20 = bf16[2,128,512]{2,1,0:T(8,128)(2,1)} copy(bf16[2,128,512]{2,1,0:T(8,128)(2,1)} %bitcast.6) | data formatting | bytes 524288
  127.6 1.6 %copy.21 = bf16[256,256]{1,0:T(8,128)(2,1)} copy(bf16[256,256]{1,0:T(8,128)(2,1)} %get-tuple-element.26) | data formatting | bytes 262144
  129.2 1.6 %copy.22 = bf16[256,256]{1,0:T(8,128)(2,1)} copy(bf16[256,256]{1,0:T(8,128)(2,1)} %get-tuple-element.27) | data formatting | bytes 262144
  130.8 1.6 %copy.23 = bf16[256,256]{1,0:T(8,128)(2,1)} copy(bf16[256,256]{1,0:T(8,128)(2,1)} %get-tuple-element.28) | data formatting | bytes 262144
  132.3 1.6 %copy.24 = bf16[256,256]{1,0:T(8,128)(2,1)} copy(bf16[256,256]{1,0:T(8,128)(2,1)} %get-tuple-element.29) | data formatting | bytes 262144

commit v3 on v2

--- a/solution.py
+++ b/solution.py
@@ -135,16 +135,8 @@
     return add
 
 
-def add_lead(dst, refs):
-    def body(i, carry):
-        dst[i] = summed(refs, i).astype(dst.dtype)
-        return carry
-
-    lax.fori_loop(0, dst.shape[0], body, 0)
-
-
 def kernel(
-    first_ref,
+    allowed_ref,
     tok_ref,
     wq_hbm,
     wk_hbm,
@@ -168,20 +160,27 @@
     xt_all,
     qkv_acc,
     do_acc,
-    q_own,
-    do_own,
+    low,
+    pieces,
+    cot_pieces,
     kv,
+    cots,
     prob,
+    mix_acc,
+    mix_here,
+    mix_in,
+    dq_here,
+    dq_in,
     mixed,
     mixed_sib,
     grads,
     grads_sib,
     kv_mate,
     kv_mate_in,
+    dkv_parts,
+    dkv_in,
     att_parts,
     att_in,
-    dkv_parts,
-    dkv_in,
     dtok_parts,
     dtok_in,
     wo_parts,
@@ -232,11 +231,8 @@
         copy.start()
 
     barrier = pltpu.get_barrier_semaphore()
-    neighbours = [
-        at(ring, pair)
-        for at in (tp_peer, ctx_peer)
-        for ring, pair in ((0, 1), (1, 0), (2, 0), (3, 0))
-    ] + [mate]
+    neighbours = [tp_peer(ring, pair) for ring, pair in ((0, 1), (1, 0), (2, 0), (3, 0))]
+    neighbours += [ctx_peer(*offset) for offset in ORDER[:7]] + [mate]
     for device in neighbours:
         pl.semaphore_signal(barrier, inc=1, device_id=device, device_id_type=MESH)
     pl.semaphore_wait(barrier, len(neighbours))
@@ -252,10 +248,27 @@
             lambda to_ring, to_pair, ring, pair: slots.at[tp_at(ring, pair)],
         )
 
-    def ctx_landing(to_ring, to_pair, ring, pair):
-        return kv.at[0, INDEX[((ring - to_ring) % 4, (pair + to_pair) % 2)]]
+    def turn(ring):
+        return (y + ring) % 4
+
+    def exchange(source, target):
+        return [
+            copies.start(source(turn(ring)), target, ctx_peer(ring, 0)) for ring in (1, 2, 3)
+        ]
+
+    def arrived(started):
+        for copy in started:
+            copy.wait_recv()
+
+    for b in range(2):
+        seen = allowed_ref[b, 0]
+        for k in range(1, 16):
+            seen = seen + allowed_ref[b, k]
+        start = (ctx + 1 - seen) * (128 // FRAME)
+        low[y, b] = jnp.full((8, 128), start.astype(F32))
 
     tokens = tp_gather(tok_ref, x_all)
+    lows = exchange(lambda to: low.at[y], low.at[y])
 
     def project(slot, first=False):
         x = x_all[slot]
@@ -287,34 +300,30 @@
     tokens.far_pair.wait_recv()
     project(tp_at(2, 1))
 
-    own_kv = kv.at[0, INDEX[(0, 0)]]
     for p in range(4):
         b, h = p // 2, p % 2
         rows = slice(b * 128, (b + 1) * 128)
-        q_own[p] = qkv_acc[rows, h * 128 : (h + 1) * 128].astype(BF)
-        own_kv[2 * p] = qkv_acc[rows, half + h * 128 : half + (h + 1) * 128].astype(BF)
-        own_kv[2 * p + 1] = qkv_acc[
-            rows, 2 * half + h * 128 : 2 * half + (h + 1) * 128
-        ].astype(BF)
-
-    rows_kv = Gather(
-        copies, ctx_peer, own_kv, lambda ring, pair: kv.at[0, INDEX[(ring, pair)]], ctx_landing
-    )
-    shared = []
-
-    def share(ring, pair):
-        k = INDEX[(ring, pair)]
-        shared.append(copies.start(kv.at[0, k], kv.at[1, k], mate))
-
-    share(0, 0)
+        for place, which in enumerate((1, 2, 0)):
+            at = which * half + h * 128
+            pieces[p, place] = qkv_acc[rows, at : at + 128].astype(BF)
+
+    from_side = [
+        copies.start(pieces.at[turn(ring), pl.ds(0, 2)], kv.at[y, 0, 1, pl.ds(0, 2)], ctx_peer(ring, 1))
+        for ring in range(4)
+    ]
+    from_rows = exchange(lambda to: pieces.at[to], kv.at[y, 0, 0])
+    kv[y, 0, 0] = pieces[y]
+
+    def share(side):
+        return copies.start(
+            kv.at[:, 0, side, pl.ds(0, 2)], kv.at[:, 1, side, pl.ds(0, 2)], mate
+        )
+
     other_half = pl.ds(pl.multiple_of((1 - core) * half, half), half)
     my_half = pl.ds(pl.multiple_of(core * half, half), half)
     x_half = copies.start(x_all.at[:, :, other_half], x_sib, mate)
     local[5].wait()
     cotangents.forward_pair()
-    rows_kv.forward_pair()
-    share(0, 1)
-    cotangents.forward_far()
     x_half.wait_recv()
 
     def transpose_block(k, carry):
@@ -323,8 +332,62 @@
         return carry
 
     lax.fori_loop(0, 8, transpose_block, 0)
-    rows_kv.forward_far()
-    share(2, 0)
+    arrived(from_rows)
+    shared = [share(0)]
+    arrived(from_side)
+    shared.append(share(1))
+    cotangents.forward_far()
+    arrived(shared)
+    arrived(lows)
+
+    key_frame = lax.broadcasted_iota(jnp.int32, (128, 128), 0) // FRAME
+    frame_gap = key_frame - lax.broadcasted_iota(jnp.int32, (128, 128), 1) // FRAME
+    frames = 128 // FRAME
+    sides = [(d, side) for d in range(2) for side in range(2)]
+    place_of = {
+        (d, side): 2 * ((xh + side) % 2) + (core if d == 0 else 1 - core) for d, side in sides
+    }
+    queries = kv[:, 0, 0, 2].reshape(512, HEAD_DIM)
+    batch_here = y // 2
+    lowest = jnp.concatenate([low[k, batch_here][0:1] for k in range(4)], axis=1)
+    tops = [[] for _ in range(4)]
+    for ys in range(4):
+        for n, (d, side) in enumerate(sides):
+            rows = slice(n * 128, (n + 1) * 128)
+            logits = dot_nt(kv[ys, d, side, 0], queries[ys * 128 :]) * scale
+            place = place_of[d, side]
+            begin = ((4 * ys + place) * frames).astype(F32)
+            logits = logits + jnp.where(lowest[:, ys * 128 :] <= begin, 0.0, -jnp.inf)
+            ahead = (place_of[0, 0] - place) * frames
+            for k in range(ys, 4):
+                part = logits[:, (k - ys) * 128 : (k - ys + 1) * 128]
+                if k == ys:
+                    part = jnp.where(frame_gap <= ahead, part, -jnp.inf)
+                prob[ys, rows, k * 128 : (k + 1) * 128] = part
+                tops[k].append(jnp.max(part, axis=0, keepdims=True))
+    top = jnp.concatenate([functools.reduce(jnp.maximum, t) for t in tops], axis=1)
+    totals = [jnp.zeros((1, 128), F32)] * 4
+    for ys in range(4):
+        for n in range(4):
+            rows = slice(n * 128, (n + 1) * 128)
+            exponent = jnp.exp(prob[ys, rows, ys * 128 :] - top[:, ys * 128 :])
+            prob[ys, rows, ys * 128 :] = exponent
+            sums = jnp.sum(exponent, axis=0, keepdims=True)
+            for k in range(ys, 4):
+                totals[k] = totals[k] + sums[:, (k - ys) * 128 : (k - ys + 1) * 128]
+    inverse = 1.0 / jnp.concatenate(totals, axis=1)
+    for ys in range(4):
+        weights = prob[ys, :, ys * 128 :] * inverse[:, ys * 128 :]
+        prob[ys, :, ys * 128 :] = weights
+        values = kv[ys, :, :, 1].reshape(512, HEAD_DIM)
+        term = dot_tn(weights.astype(BF), values)
+        if ys == 0:
+            mix_acc[...] = term
+        else:
+            mix_acc[ys * 128 :] += term
+    mix_here[...] = mix_acc[...].astype(BF).reshape(4, 128, HEAD_DIM)
+    from_mix = exchange(lambda to: mix_here.at[to], mix_in.at[y])
+    mix_in[y] = mix_here[y]
     cotangents.up.wait_recv()
     cotangents.down.wait_recv()
     local[4].wait()
@@ -340,10 +403,6 @@
     pull_back(tp, first=True)
     for offset in ((0, 1), (2, 0), (1, 0), (3, 0)):
         pull_back(tp_at(*offset))
-    rows_kv.up.wait_recv()
-    share(3, 0)
-    rows_kv.down.wait_recv()
-    share(1, 0)
     cotangents.up_pair.wait_recv()
     cotangents.down_pair.wait_recv()
     pull_back(tp_at(1, 1))
@@ -353,60 +412,17 @@
     g_half = copies.start(g_all.at[:, :, other_half], g_sib, mate)
     for p in range(4):
         b, h = p // 2, p % 2
-        do_own[p] = do_acc[b * 128 : (b + 1) * 128, h * 128 : (h + 1) * 128].astype(BF)
-    rows_kv.up_pair.wait_recv()
-    share(3, 1)
-    rows_kv.down_pair.wait_recv()
-    share(1, 1)
-    rows_kv.far_pair.wait_recv()
-    share(2, 1)
-    for copy in shared:
-        copy.wait_recv()
-
-    key_frame = lax.broadcasted_iota(jnp.int32, (128, 128), 0) // FRAME
-    frame_gap = key_frame - lax.broadcasted_iota(jnp.int32, (128, 128), 1) // FRAME
-    frames = 128 // FRAME
-    blocks = [
-        [2 * chip_at(*ORDER[k]) + (core if d == 0 else 1 - core) for k in range(8)]
-        for d in range(2)
-    ]
-
-    def forward(p, carry):
-        b = p // 2
-        q = q_own[p]
-        lowest = first_ref[b]
-        tops = []
-        for d in range(2):
-            keys = kv[d, :, 2 * p].reshape(8 * 128, HEAD_DIM)
-            logits = (dot_nt(keys, q) * scale).reshape(8, 128, 128)
-            for k in range(8):
-                block = blocks[d][k]
-                visible = (frame_gap <= (ctx - block) * frames) & (
-                    key_frame >= (lowest - block) * frames
-                )
-                masked = jnp.where(visible, logits[k], -jnp.inf)
-                prob[p, d, k] = masked
-                tops.append(jnp.max(masked, axis=0, keepdims=True))
-        top = functools.reduce(jnp.maximum, tops)
-        total = jnp.zeros((1, 128), F32)
-        for d in range(2):
-            for k in range(8):
-                exponent = jnp.exp(prob[p, d, k] - top)
-                prob[p, d, k] = exponent
-                total = total + jnp.sum(exponent, axis=0, keepdims=True)
-        inverse = 1.0 / total
-        out = jnp.zeros((128, HEAD_DIM), F32)
-        for d in range(2):
-            weights = prob[p, d] * inverse
-            prob[p, d] = weights
-            values = kv[d, :, 2 * p + 1].reshape(8 * 128, HEAD_DIM)
-            out = out + dot_tn(weights.reshape(8 * 128, 128).astype(BF), values)
-        rows = pl.ds(pl.multiple_of(b * 128, 128), 128)
-        columns = pl.ds(pl.multiple_of((p % 2) * 128, 128), 128)
-        mixed[rows, columns] = out.astype(BF)
-        return carry
-
-    lax.fori_loop(0, 4, forward, 0)
+        cot_pieces[p] = do_acc[b * 128 : (b + 1) * 128, h * 128 : (h + 1) * 128].astype(BF)
+    from_cots = exchange(lambda to: cot_pieces.at[to], cots.at[y])
+    cots[y] = cot_pieces[y]
+
+    def assemble(target, arrivals):
+        for p in range(4):
+            b, h = p // 2, p % 2
+            target[b * 128 : (b + 1) * 128, h * 128 : (h + 1) * 128] = arrivals[p]
+
+    arrived(from_mix)
+    assemble(mixed, mix_in)
 
     mixed_copy = copies.start(mixed, mixed_sib, mate)
     attended = Scatter(copies, tp_peer, att_parts, att_in, add_rows(64))
@@ -431,44 +447,54 @@
         if k < 5:
             out_grads.send(k)
 
-    def backward(d, out):
-        def body(p, carry):
-            rows = pl.ds(pl.multiple_of((p // 2) * 128, 128), 128)
-            columns = pl.ds(pl.multiple_of((p % 2) * 128, 128), 128)
-            q, do = q_own[p], do_own[p]
-            inner = lax.dot_general(
-                jnp.ones((8, HEAD_DIM), F32),
-                do.astype(F32) * mixed[rows, columns].astype(F32),
-                (((1,), (1,)), ((), ())),
-                precision=lax.Precision.HIGHEST,
-                preferred_element_type=F32,
-            )[0:1]
-            keys = kv[d, :, 2 * p].reshape(8 * 128, HEAD_DIM)
-            values = kv[d, :, 2 * p + 1].reshape(8 * 128, HEAD_DIM)
-            weights = prob[p, d].reshape(8 * 128, 128)
-            slopes = (weights * (dot_nt(values, do) - inner) * scale).astype(BF)
-            out[:, 2 * p] = dot(slopes, q).astype(BF).reshape(8, 128, HEAD_DIM)
-            out[:, 2 * p + 1] = dot(weights.astype(BF), do).astype(BF).reshape(8, 128, HEAD_DIM)
-            term = dot_tn(slopes, keys)
-            if d == 1:
-                do_acc[rows, columns] = term
-            else:
-                do_acc[rows, columns] += term
-            return carry
-
-        lax.fori_loop(0, 4, body, 0)
-
-    backward(1, kv_mate)
-    mate_copy = copies.start(kv_mate, kv_mate_in, mate)
-    backward(0, dkv_parts)
-    grads[:, :half] = do_acc[...].astype(BF)
+    arrived(from_cots)
+    cot_rows = cots[...].reshape(512, HEAD_DIM)
+    inner = lax.dot_general(
+        jnp.ones((8, HEAD_DIM), F32),
+        cot_rows.astype(F32) * mix_here[...].reshape(512, HEAD_DIM).astype(F32),
+        (((1,), (1,)), ((), ())),
+        precision=lax.Precision.HIGHEST,
+        preferred_element_type=F32,
+    )[0:1]
+    mate_copies = []
+    for ys in range(4):
+        keys = kv[ys, :, :, 0].reshape(512, HEAD_DIM)
+        values = kv[ys, :, :, 1].reshape(512, HEAD_DIM)
+        weights = prob[ys, :, ys * 128 :]
+        slopes = (
+            weights * (dot_nt(values, cot_rows[ys * 128 :]) - inner[:, ys * 128 :]) * scale
+        ).astype(BF)
+        key_part = dot(slopes, queries[ys * 128 :]).astype(BF).reshape(2, 2, 128, HEAD_DIM)
+        value_part = (
+            dot(weights.astype(BF), cot_rows[ys * 128 :]).astype(BF).reshape(2, 2, 128, HEAD_DIM)
+        )
+        dkv_parts[ys, :, 0] = key_part[0]
+        dkv_parts[ys, :, 1] = value_part[0]
+        kv_mate[ys, :, 0] = key_part[1]
+        kv_mate[ys, :, 1] = value_part[1]
+        mate_copies.append(copies.start(kv_mate.at[ys], kv_mate_in.at[ys], mate))
+        term = dot_tn(slopes, keys)
+        if ys == 0:
+            mix_acc[...] = term
+        else:
+            mix_acc[ys * 128 :] += term
+    dq_here[...] = mix_acc[...].astype(BF).reshape(4, 128, HEAD_DIM)
+    from_dq = exchange(lambda to: dq_here.at[to], dq_in.at[y])
+    dq_in[y] = dq_here[y]
+    for ys in range(4):
+        mate_copies[ys].wait_recv()
+        for side in range(2):
+            dkv_parts[ys, side] = summed((dkv_parts, kv_mate_in), (ys, side)).astype(BF)
+    from_dkv = [
+        copies.start(dkv_parts.at[turn(ring), side], dkv_in.at[y, side], ctx_peer(ring, side))
+        for ring in (2, 1, 3, 0)
+        for side in (1, 0)
+        if (ring, side) != (0, 0)
+    ]
+    dkv_in[y, 0] = dkv_parts[y, 0]
+    arrived(from_dq)
+    assemble(grads, dq_in)
     dq_copy = copies.start(grads.at[:, pl.ds(0, half)], grads_sib.at[:, pl.ds(0, half)], mate)
-    mate_copy.wait_recv()
-    kv_sums = Scatter(copies, ctx_peer, dkv_parts, dkv_in, add_lead)
-    for k in range(8):
-        add_lead(dkv_parts.at[k], (dkv_parts.at[k], kv_mate_in.at[k]))
-        if k < 5:
-            kv_sums.send(k)
     attended.relay_far()
     attended.relay_pair()
     out_grads.relay_far()
@@ -485,8 +511,6 @@
         if k < 5 and k != 0:
             query_grads.send(k)
     query_grads.send(0)
-    kv_sums.relay_far()
-    kv_sums.relay_pair()
 
     def store_rows(out):
         return lambda refs: add_rows(64)(out, refs)
@@ -494,16 +518,14 @@
     attended.finish(store_rows(att_out))
     out_grads.finish(store_rows(go_out))
 
-    def store_kv(refs):
-        for p in range(4):
-            b, h = p // 2, p % 2
-            for which in range(2):
-                at = (1 + which) * half + h * 128
-                grads[b * 128 : (b + 1) * 128, at : at + 128] = summed(
-                    refs, 2 * p + which
-                ).astype(BF)
-
-    kv_sums.finish(store_kv)
+    arrived(from_dkv)
+    for p in range(4):
+        b, h = p // 2, p % 2
+        for which in range(2):
+            at = (1 + which) * half + h * 128
+            grads[b * 128 : (b + 1) * 128, at : at + 128] = summed(
+                (dkv_in.at[:, 0], dkv_in.at[:, 1]), (p, which)
+            ).astype(BF)
     kv_columns = pl.ds(half, 2 * half)
     dkv_copy = copies.start(grads.at[:, kv_columns], grads_sib.at[:, kv_columns], mate)
 
@@ -551,14 +573,26 @@
     copies.finish()
 
 
-N_COPIES = 3 * GATHER_COPIES + 6 * SCATTER_COPIES + 8 + 6
+def settle(*refs):
+    sources, results, held, sems = refs[:6], refs[6:12], refs[12:18], refs[18]
+    reads = [pltpu.make_async_copy(sources[k], held[k], sems.at[k]) for k in range(6)]
+    writes = [pltpu.make_async_copy(held[k], results[k], sems.at[6 + k]) for k in range(6)]
+    for read in reads:
+        read.start()
+    for read, write in zip(reads, writes):
+        read.wait()
+        write.start()
+    for write in writes:
+        write.wait()
+
+
+N_COPIES = 2 * GATHER_COPIES + 5 * SCATTER_COPIES + 26 + 2 + 4 + 5
 
 
 def per_device(tokens, w_query, w_key, w_value, w_out, allowed, grad_out):
     batch, block, width = tokens.shape
     rows = batch * block
     head_width = w_query.shape[1]
-    first = lax.axis_index("ctx") + 1 - jnp.sum(allowed[:, 0, :], axis=1, dtype=jnp.int32)
     vmem = pl.BlockSpec(memory_space=pltpu.VMEM)
     hbm = pl.BlockSpec(memory_space=pl.ANY)
 
@@ -586,18 +620,26 @@
             halves(8, 256, 512),
             pltpu.VMEM((256, 768), F32),
             pltpu.VMEM((256, 256), F32),
+            pltpu.VMEM((4, 2, 8, 128), F32),
+            halves(4, 3, 128, 128),
+            halves(4, 128, 128),
+            halves(4, 2, 2, 3, 128, 128),
+            halves(4, 128, 128),
+            pltpu.VMEM((4, 512, 512), F32),
+            pltpu.VMEM((512, 128), F32),
             halves(4, 128, 128),
             halves(4, 128, 128),
-            halves(2, 8, 8, 128, 128),
-            pltpu.VMEM((4, 2, 8, 128, 128), F32),
+            halves(4, 128, 128),
+            halves(4, 128, 128),
             halves(256, 256),
             halves(256, 256),
             halves(256, 768),
             halves(256, 768),
-            halves(8, 8, 128, 128),
-            halves(8, 8, 128, 128),
+            halves(4, 2, 2, 128, 128),
+            halves(4, 2, 2, 128, 128),
+            halves(4, 2, 2, 128, 128),
+            halves(4, 2, 2, 128, 128),
             *pair(256, 512),
-            *pair(8, 128, 128),
             *pair(256, 512),
             *pair(256, 256),
             *pair(256, 256),
@@ -610,7 +652,7 @@
             collective_id=0, has_side_effects=True, vmem_limit_bytes=60 * 2**20
         ),
     )(
-        first,
+        allowed.reshape(batch, allowed.shape[2]),
         tokens.reshape(rows, width),
         w_query,
         w_key,
@@ -618,7 +660,14 @@
         w_out,
         grad_out.reshape(rows, width),
     )
-    attended, grad_tokens, *weight_grads = outs
+    attended, grad_tokens, *weight_grads = pl.pallas_call(
+        settle,
+        out_shape=[jax.ShapeDtypeStruct(out.shape, out.dtype) for out in outs],
+        in_specs=[hbm] * 6,
+        out_specs=[hbm] * 6,
+        scratch_shapes=[pltpu.VMEM(out.shape, out.dtype) for out in outs]
+        + [pltpu.SemaphoreType.DMA((12,))],
+    )(*outs)
     return (
         attended.reshape(batch, block, width),
         grad_tokens.reshape(batch, block, width),

time: 135 us -> 109 us (0.81)
  Pallas kernels: 122 us -> 107 us
  local copies, waits for them, and re-layouts: 9.61 us -> 0 us
    pallas_call x1, Pallas kernels: 122 us -> 105 us  [per_device(): pl.pallas_call(kernel, out_shape=[jax.ShapeDtypeStruct((rows, width), BF)...]
    unnamed x6 -> x0, local copies, waits for them, and re-layouts: 9.61 us -> none
    pallas_call x0 -> x1, Pallas kernels: none -> 2.01 us  [per_device(): pl.pallas_call(settle, out_shape=[jax.ShapeDtypeStruct(out.shape, out.dty...]
where the time goes in v3:
time: 109 us; the launch traced here: 107 us
  Pallas kernels  107 us (98%)
    pallas_call x1, Pallas kernels, per_device(): pl.pallas_call(kernel, out_shape=[jax.ShapeDtypeStruct((rows, width), BF)...  105 us

profile of v3, /device:TPU:1, one launch (start us, length us, event | category | flops | bytes accessed | tf_op | source)
XLA Modules:
  0.0 107.2 jit_solution(6965314634308921993)
XLA Ops:
  0.6 104.6 %shard_map.118 = (bf16[256,512]{1,0:T(8,128)(2,1)}, bf16[256,512]{1,0:T(8,128)(2,1)}, bf16[256,256]{1,0:T(8,128)(2,1)}, bf16[256,256]{1,0:T(8,128)(2,1)}, bf16[2...) custom-call(s32[2,16]{1,0:T(2,128)} %bitcast.7, bf16[256,512]{1,0:T(8,128)(2,1)} %bitcast.5, bf16[4096,256]{1,0:T(8,128)(2,1)} %wq_hbm.1, ...), custom_call_target="tpu_custom_call" | custom-call | tf_op jit(solution)/shard_map/pallas_call | solution.py:605
  105.2 2.0 %shard_map.119 = (bf16[256,512]{1,0:T(8,128)(2,1)}, bf16[256,512]{1,0:T(8,128)(2,1)}, bf16[256,256]{1,0:T(8,128)(2,1)}, bf16[256,256]{1,0:T(8,128)(2,1)}, bf16[2...) custom-call(bf16[256,512]{1,0:T(8,128)(2,1)} %get-tuple-element.18.refs_0_, bf16[256,512]{1,0:T(8,128)(2,1)} %get-tuple-element.19.refs_1_, ...), custom_call_target="tpu_custom_call" | custom-call | tf_op jit(solution)/shard_map/pallas_call | solution.py:663

commit v4 on v3

--- a/solution.py
+++ b/solution.py
@@ -13,10 +13,9 @@
 BF = jnp.bfloat16
 F32 = jnp.float32
 
-ORDER = ((2, 1), (1, 1), (3, 1), (1, 0), (3, 0), (2, 0), (0, 1), (0, 0))
-INDEX = {offset: k for k, offset in enumerate(ORDER)}
+ORDER = ((2, 1), (1, 1), (3, 1), (2, 0), (1, 0), (3, 0), (0, 1), (0, 0))
 GATHER_COPIES = 7
-SCATTER_COPIES = 7
+SCATTER_COPIES = 13
 
 
 def dot(a, b):
@@ -82,38 +81,49 @@
 class Scatter:
     def __init__(self, copies, peer, parts, landed, add):
         self.copies, self.peer, self.parts, self.landed, self.add = copies, peer, parts, landed, add
+        rows = parts.shape[1] // 2
+        self.low, self.high = pl.ds(0, rows), pl.ds(rows, rows)
+        self.far, self.near = [[], []], [[], []]
+
+    def move(self, k, slot, rows, ring):
+        return self.copies.start(
+            self.parts.at[k, rows], self.landed.at[slot, rows], self.peer(ring, 0)
+        )
 
     def send(self, k):
+        if k >= 6:
+            return
         ring, pair = ORDER[k]
-        to = self.peer(0, 1) if ring == 2 else self.peer(ring, 0)
-        copy = self.copies.start(self.parts.at[k], self.landed.at[k], to)
-        setattr(self, ("far_pair", "up_pair", "down_pair", "up", "down")[k], copy)
-
-    def relay_far(self):
-        self.far_pair.wait_recv()
-        self.add(self.parts.at[5], (self.parts.at[5], self.landed.at[0]))
-        self.far = self.copies.start(self.parts.at[5], self.landed.at[5], self.peer(2, 0))
-
-    def relay_pair(self):
-        self.up_pair.wait_recv()
-        self.down_pair.wait_recv()
-        self.add(
-            self.parts.at[6], (self.parts.at[6], self.landed.at[1], self.landed.at[2])
-        )
-        self.pair = self.copies.start(self.parts.at[6], self.landed.at[6], self.peer(0, 1))
+        slot = 3 * pair
+        if ring == 2:
+            self.far[pair] = [self.move(k, slot, self.low, 1), self.move(k, slot, self.high, 3)]
+        elif ring == 1:
+            self.near[pair].append(self.move(k, slot + 1, self.high, 1))
+        else:
+            self.near[pair].append(self.move(k, slot + 2, self.low, 3))
+
+    def relay(self):
+        for pair in (1, 0):
+            first, slot = 3 - 3 * pair, 3 * pair
+            for copy, k, to, rows, ring in (
+                (self.far[pair][0], first + 1, slot + 1, self.low, 1),
+                (self.far[pair][1], first + 2, slot + 2, self.high, 3),
+            ):
+                copy.wait_recv()
+                part = self.parts.at[k, rows]
+                self.add(part, (part, self.landed.at[slot, rows]))
+                self.near[pair].append(self.move(k, to, rows, ring))
+
+    def cross(self):
+        for copy in self.near[1]:
+            copy.wait_recv()
+        self.add(self.parts.at[6], (self.parts.at[6], self.landed.at[4], self.landed.at[5]))
+        self.over = self.copies.start(self.parts.at[6], self.landed.at[6], self.peer(0, 1))
 
     def finish(self, store):
-        for copy in (self.up, self.down, self.far, self.pair):
+        for copy in self.near[0] + [self.over]:
             copy.wait_recv()
-        store(
-            (
-                self.parts.at[7],
-                self.landed.at[3],
-                self.landed.at[4],
-                self.landed.at[5],
-                self.landed.at[6],
-            )
-        )
+        store((self.parts.at[7], self.landed.at[1], self.landed.at[2], self.landed.at[6]))
 
 
 def summed(refs, where):
@@ -433,8 +443,7 @@
 
     for k in range(8):
         out_part(k)
-        if k < 5:
-            attended.send(k)
+        attended.send(k)
     mixed_copy.wait_recv()
     g_half.wait_recv()
 
@@ -444,8 +453,7 @@
         wo_parts[k] = (
             dot_tn(mixed[...], g_all[chip, :, my_half]) + dot_tn(mixed_sib[...], g_sib[chip])
         ).astype(BF)
-        if k < 5:
-            out_grads.send(k)
+        out_grads.send(k)
 
     arrived(from_cots)
     cot_rows = cots[...].reshape(512, HEAD_DIM)
@@ -495,10 +503,8 @@
     arrived(from_dq)
     assemble(grads, dq_in)
     dq_copy = copies.start(grads.at[:, pl.ds(0, half)], grads_sib.at[:, pl.ds(0, half)], mate)
-    attended.relay_far()
-    attended.relay_pair()
-    out_grads.relay_far()
-    out_grads.relay_pair()
+    attended.relay()
+    out_grads.relay()
 
     dq_copy.wait_recv()
     query_grads = Scatter(copies, ctx_peer, wq_parts, wq_in, add_rows(64))
@@ -508,15 +514,10 @@
             dot(xt_all[chip, :, :half], grads[:, :half])
             + dot(xt_all[chip, :, half:], grads_sib[:, :half])
         ).astype(BF)
-        if k < 5 and k != 0:
-            query_grads.send(k)
-    query_grads.send(0)
+        query_grads.send(k)
 
     def store_rows(out):
         return lambda refs: add_rows(64)(out, refs)
-
-    attended.finish(store_rows(att_out))
-    out_grads.finish(store_rows(go_out))
 
     arrived(from_dkv)
     for p in range(4):
@@ -528,6 +529,9 @@
             ).astype(BF)
     kv_columns = pl.ds(half, 2 * half)
     dkv_copy = copies.start(grads.at[:, kv_columns], grads_sib.at[:, kv_columns], mate)
+    query_grads.relay()
+    attended.cross()
+    out_grads.cross()
 
     token_grads = Scatter(copies, tp_peer, dtok_parts, dtok_in, add_rows(64))
     for k in range(8):
@@ -537,8 +541,7 @@
             + dot_nt(grads[:, half : 2 * half], wk[rows, :])
             + dot_nt(grads[:, 2 * half :], wv[rows, :])
         ).astype(BF)
-        if k < 5:
-            token_grads.send(k)
+        token_grads.send(k)
 
     dkv_copy.wait_recv()
     kv_grads = Scatter(copies, ctx_peer, wkv_parts, wkv_in, add_rows(64))
@@ -548,14 +551,14 @@
             dot(xt_all[chip, :, :half], grads[:, half:])
             + dot(xt_all[chip, :, half:], grads_sib[:, half:])
         ).astype(BF)
-        if k < 5:
-            kv_grads.send(k)
-    query_grads.relay_far()
-    query_grads.relay_pair()
-    token_grads.relay_far()
-    token_grads.relay_pair()
-    kv_grads.relay_far()
-    kv_grads.relay_pair()
+        kv_grads.send(k)
+    query_grads.cross()
+    token_grads.relay()
+    kv_grads.relay()
+    attended.finish(store_rows(att_out))
+    out_grads.finish(store_rows(go_out))
+    token_grads.cross()
+    kv_grads.cross()
     query_grads.finish(store_rows(gq_out))
     token_grads.finish(store_rows(dtok_out))
 

time: 109 us -> 107 us (0.982)
  Pallas kernels: 107 us -> 105 us
    pallas_call x1, Pallas kernels: 105 us -> 103 us  [per_device(): pl.pallas_call(kernel, out_shape=[jax.ShapeDtypeStruct((rows, width), BF)...]
where the time goes in v4:
time: 107 us; the launch traced here: 105 us
  Pallas kernels  105 us (98%)
    pallas_call x1, Pallas kernels, per_device(): pl.pallas_call(kernel, out_shape=[jax.ShapeDtypeStruct((rows, width), BF)...  103 us

profile of v4, /device:TPU:1, one launch (start us, length us, event | category | flops | bytes accessed | tf_op | source)
XLA Modules:
  0.0 105.3 jit_solution(15732871742013301384)
XLA Ops:
  0.6 102.7 %shard_map.118 = (bf16[256,512]{1,0:T(8,128)(2,1)}, bf16[256,512]{1,0:T(8,128)(2,1)}, bf16[256,256]{1,0:T(8,128)(2,1)}, bf16[256,256]{1,0:T(8,128)(2,1)}, bf16[2...) custom-call(s32[2,16]{1,0:T(2,128)} %bitcast.7, bf16[256,512]{1,0:T(8,128)(2,1)} %bitcast.5, bf16[4096,256]{1,0:T(8,128)(2,1)} %wq_hbm.1, ...), custom_call_target="tpu_custom_call" | custom-call | tf_op jit(solution)/shard_map/pallas_call | solution.py:608
  103.3 2.0 %shard_map.119 = (bf16[256,512]{1,0:T(8,128)(2,1)}, bf16[256,512]{1,0:T(8,128)(2,1)}, bf16[256,256]{1,0:T(8,128)(2,1)}, bf16[256,256]{1,0:T(8,128)(2,1)}, bf16[2...) custom-call(bf16[256,512]{1,0:T(8,128)(2,1)} %get-tuple-element.18.refs_0_, bf16[256,512]{1,0:T(8,128)(2,1)} %get-tuple-element.19.refs_1_, ...), custom_call_target="tpu_custom_call" | custom-call | tf_op jit(solution)/shard_map/pallas_call | solution.py:666

commit v5 on v4

--- a/solution.py
+++ b/solution.py
@@ -135,12 +135,9 @@
 
 def add_rows(step):
     def add(dst, refs):
-        def body(i, carry):
-            where = (pl.ds(pl.multiple_of(i * step, step), step), slice(None))
+        for at in range(0, dst.shape[0], step):
+            where = (pl.ds(at, step), slice(None))
             dst[where] = summed(refs, where).astype(dst.dtype)
-            return carry
-
-        lax.fori_loop(0, dst.shape[0] // step, body, 0)
 
     return add
 
@@ -295,11 +292,11 @@
         copy.wait()
     project(tp, first=True)
     tokens.forward_pair()
+    cotangents = tp_gather(gout_ref, g_all)
     project(tp_at(0, 1))
     tokens.forward_far()
     tokens.up.wait_recv()
     tokens.down.wait_recv()
-    cotangents = tp_gather(gout_ref, g_all)
     project(tp_at(2, 0))
     project(tp_at(1, 0))
     project(tp_at(3, 0))
@@ -552,11 +549,11 @@
             + dot(xt_all[chip, :, half:], grads_sib[:, half:])
         ).astype(BF)
         kv_grads.send(k)
-    query_grads.cross()
-    token_grads.relay()
-    kv_grads.relay()
     attended.finish(store_rows(att_out))
     out_grads.finish(store_rows(go_out))
+    token_grads.relay()
+    query_grads.cross()
+    kv_grads.relay()
     token_grads.cross()
     kv_grads.cross()
     query_grads.finish(store_rows(gq_out))

time: 107 us -> 106 us (level)
  no operation moved by 1% of the time
where the time goes in v5:
time: 106 us; the launch traced here: 105 us
  Pallas kernels  104 us (98%)
    pallas_call x1, Pallas kernels, per_device(): pl.pallas_call(kernel, out_shape=[jax.ShapeDtypeStruct((rows, width), BF)...  102 us

profile of v5, /device:TPU:1, one launch (start us, length us, event | category | flops | bytes accessed | tf_op | source)
XLA Modules:
  0.0 105.0 jit_solution(107160351461768928)
XLA Ops:
  0.6 102.4 %shard_map.118 = (bf16[256,512]{1,0:T(8,128)(2,1)}, bf16[256,512]{1,0:T(8,128)(2,1)}, bf16[256,256]{1,0:T(8,128)(2,1)}, bf16[256,256]{1,0:T(8,128)(2,1)}, bf16[2...) custom-call(s32[2,16]{1,0:T(2,128)} %bitcast.7, bf16[256,512]{1,0:T(8,128)(2,1)} %bitcast.5, bf16[4096,256]{1,0:T(8,128)(2,1)} %wq_hbm.1, ...), custom_call_target="tpu_custom_call" | custom-call | tf_op jit(solution)/shard_map/pallas_call | solution.py:605
  103.0 2.0 %shard_map.119 = (bf16[256,512]{1,0:T(8,128)(2,1)}, bf16[256,512]{1,0:T(8,128)(2,1)}, bf16[256,256]{1,0:T(8,128)(2,1)}, bf16[256,256]{1,0:T(8,128)(2,1)}, bf16[2...) custom-call(bf16[256,512]{1,0:T(8,128)(2,1)} %get-tuple-element.18.refs_0_, bf16[256,512]{1,0:T(8,128)(2,1)} %get-tuple-element.19.refs_1_, ...), custom_call_target="tpu_custom_call" | custom-call | tf_op jit(solution)/shard_map/pallas_call | solution.py:663
